TPU v7x, 32 devices: a whole 2x2x4 slice. The times are simulated.
32 devices in a mesh: obl: 8 (over z, y), scn: 4 (over x, core).
Axes of the slice: x: 2, y: 2, z: 4, core: 2. Of those that a mesh axis runs over, the one named last changes fastest.
Arguments:
- factors: bfloat16 [16384, 128], P('scn'), may hold values from -6 to 6
- idiosyncratic: bfloat16 [16384, 16384], P('obl', 'scn'), may hold values from -6 to 6
- loadings: bfloat16 [16384, 128], P('obl'), may hold values from -0.375 to 0.375
- rating: int32 [16384], P('obl'), may hold values from 0 to 15
- barrier: float32 [16], replicated, may hold values from 1 to 3
- loss_given: float32 [16384], P('obl'), may hold values from 0.2 to 0.9
- sector: int32 [16384], P('obl'), may hold values from 0 to 15, as said below
- allowed: int32 [256, 16], replicated, may hold values from 0 to 1, as said below
- holdings: float32 [16384, 256], P('obl'), may hold values from 0.1 to 10
Outputs:
- positions: float32 [16384, 256], P('obl')
- shortfall: float32 [2, 256], replicated
Inputs may be any that keep to these rules, and one draw needn't show every extreme that they name: Each sector holds exactly 1024 obligors. `allowed`: every mandate allows at least one sector.
All inputs are finite; a program needn't handle non-finite values.
Results may differ from a plain program's by a relative error of at most 0.0003.
Values may be sent and summed in bfloat16 or wider, within the bound.
A program may use at most 128 MiB of HBM per device.

v0:
```python
import jax
import jax.numpy as jnp
from jax import lax
from jax.sharding import PartitionSpec as P

STEPS = 2


IDIO_SCALE = 0.8
SHARP = 2.0
LEVEL = 0.99
QUANTILE = 2.326
SMOOTH = 0.5
EPSILON = 1e-06
STEP_RATE = 8.0


def tail_terms(losses, center, spread, tail_scale):
    deviation = jnp.sqrt(spread + EPSILON)
    thresh = center + QUANTILE * deviation
    smooth_width = SMOOTH * deviation
    scaled = (losses - thresh) / smooth_width
    tail_weight = (jax.nn.sigmoid(scaled) * tail_scale).astype(jnp.bfloat16)
    return (scaled, thresh, smooth_width, tail_weight)


def on_device(
    factors, idiosyncratic, loadings, rating, barrier, loss_given, sector, allowed, holdings
):
    obl_dev = idiosyncratic.shape[0]
    scn_dev = idiosyncratic.shape[1]
    obligors = obl_dev * lax.axis_size("obl")
    scenarios = scn_dev * lax.axis_size("scn")
    tail_scale = 1.0 / ((1.0 - LEVEL) * scenarios)
    sector_hot = (sector[:, None] == jnp.arange(allowed.shape[1])[None, :]).astype(jnp.float32)
    eligible = lax.dot_general(
        sector_hot,
        allowed.astype(jnp.float32),
        (((1,), (1,)), ((), ())),
        precision=lax.Precision.HIGHEST,
    )
    rating_hot = (rating[:, None] == jnp.arange(barrier.shape[0])[None, :]).astype(jnp.float32)
    barrier_rows = jnp.dot(rating_hot, barrier, precision=lax.Precision.HIGHEST)
    systematic = lax.dot_general(
        loadings, factors, (((1,), (1,)), ((), ())), preferred_element_type=jnp.float32
    )
    latent = systematic + IDIO_SCALE * idiosyncratic.astype(jnp.float32)
    default_prob = jax.nn.sigmoid((latent - barrier_rows[:, None]) * SHARP).astype(jnp.bfloat16)
    weighted = eligible * holdings
    totals = lax.psum(jnp.sum(weighted, 0), "obl")
    positions = obligors * weighted / totals
    results = []
    for iteration in range(STEPS):
        exposure = (loss_given[:, None] * positions / obligors).astype(jnp.bfloat16)
        partial_value = lax.dot_general(
            default_prob, exposure, (((0,), (0,)), ((), ())), preferred_element_type=jnp.float32
        )
        losses = lax.psum(partial_value, "obl")
        first, second = lax.psum((jnp.sum(losses, 0), jnp.sum(losses * losses, 0)), "scn")
        center = first / scenarios
        spread = second / scenarios - center * center
        scaled, thresh, smooth_width, tail_weight = tail_terms(losses, center, spread, tail_scale)
        tail_sum = lax.psum(jnp.sum(jax.nn.softplus(scaled), 0), "scn")
        results.append(thresh + smooth_width * (tail_sum * tail_scale))
        gradient = jnp.dot(default_prob, tail_weight, preferred_element_type=jnp.float32)
        gradient = lax.psum(gradient, "scn")
        gradient = loss_given[:, None] * eligible * gradient
        unnorm = positions * jnp.exp(-STEP_RATE * gradient)
        totals = lax.psum(jnp.sum(unnorm, 0), "obl")
        positions = obligors * unnorm / totals
    return (positions, jnp.stack(results))


def solution(mesh):
    return jax.shard_map(
        on_device,
        mesh=mesh,
        in_specs=(
            P("scn", None),
            P("obl", "scn"),
            P("obl", None),
            P("obl"),
            P(),
            P("obl"),
            P("obl"),
            P(),
            P("obl", None),
        ),
        out_specs=(P("obl", None), P()),
        check_vma=False,
    )
```

profile of v0, /device:TPU:0, one launch (start us, length us, event | category | flops | bytes accessed | tf_op | source)
XLA Modules:
  0.0 590.1 jit_solution(18000236785116906874)
XLA Ops:
  7.2 0.0 copy-start
  7.2 0.0 copy-start.4
  7.2 0.0 copy-start.3
  7.2 0.0 all-reduce.8.cloned.1.call-start
  7.2 2.6 multiply_reduce_fusion.2
  9.9 23.1 %psum.91 = f32[256]{0:T(256)S(1)} all-reduce(f32[256]{0:T(256)S(1)} %get-tuple-element.20), channel_id=1, replica_groups=mesh['obl'=8,'scn'=4] {'obl'}, use_global_device_ids=true, to_apply=%region_1.0 | all-reduce | flops 256 | bytes 2048 | tf_op jit(solution)/shard_map/psum | solution.py:50
  33.0 0.0 copy-done.4
  33.0 0.0 copy-done.3
  33.0 0.7 fusion.15
  33.8 0.0 copy-done
  33.8 0.0 copy-start.2
  33.8 16.5 %divide_convert_fusion = bf16[2048,4096]{1,0:T(8,128)(2,1)} fusion(bf16[2048,4096]{1,0:T(8,128)(2,1)} %param.10, f32[2048]{0:T(1024)S(1)} %bitcast.14, bf16[2048,128]{1,0:T(8,128)(2,1)} %param.11, bf16[4096,128]{1,0:T(8,128)(2,1)S(1)} %copy-done), kind=kOutput, calls=%fused_computation | convolution fusion | flops 2222981120 | bytes 35135488 | tf_op jit(solution)/shard_map/dot_general | solution.py:44
  50.3 0.0 copy-done.2
  50.3 13.6 %fusion.8 = f32[4096,256]{1,0:T(8,128)} fusion(bf16[2048,4096]{1,0:T(8,128)(2,1)} %divide_convert_fusion, f32[2048]{0:T(1024)S(1)} %copy-done.2, f32[256]{0:T(256)S(1)} %psum.91, f32[2048,256]{1,0:T(8,128)S(1)} %get-tuple-element.21, f32[2048,256]{1,0:T(8,128)} %param.17), kind=kOutput, calls=%fused_computation.24 | convolution fusion | flops 4298113024 | bytes 25175040 | tf_op jit(solution)/shard_map/dot_general | solution.py:55
  63.9 0.0 all-reduce.8.cloned.1.call-update
  63.9 0.0 all-reduce.10.cloned.1.call-start
  64.0 153.6 %all-reduce.8.cloned.1.call-done = f32[4096,256]{1,0:T(8,128)} async-done(((f32[4096,256]{1,0:T(8,128)}), f32[4096,256]{1,0:T(8,128)}) %all-reduce.8.cloned.1.call-update) | async-done | bytes 4194320 | tf_op jit(solution)/shard_map/psum | solution.py:58
  217.6 2.7 multiply_reduce_fusion.1
  220.4 7.0 %all-reduce.2 = (f32[256]{0:T(256)S(1)}, f32[256]{0:T(256)S(1)}) all-reduce(f32[256]{0:T(256)S(1)} %get-tuple-element.5, f32[256]{0:T(256)S(1)} %get-tuple-element.4), channel_id=1, replica_groups=mesh['obl'=8,'scn'=4] {'scn'}, use_global_device_ids=true, to_apply=%region_4.0 | all-reduce | flops 512 | bytes 4096 | tf_op jit(solution)/shard_map/psum | solution.py:59
  227.4 13.1 %fusion.2 = f32[2048,256]{1,0:T(8,128)} fusion(bf16[2048,4096]{1,0:T(8,128)(2,1)} %divide_convert_fusion, f32[4096,256]{1,0:T(8,128)} %all-reduce.8.cloned.1.call-done, f32[256]{0:T(256)S(1)} %get-tuple-element.19, f32[256]{0:T(256)S(1)} %get-tuple-element.18), kind=kOutput, calls=%fused_computation.11 | convolution fusion | flops 4302307328 | bytes 23070720 | tf_op jit(solution)/shard_map/dot_general | solution.py:65
  240.5 0.0 all-reduce.10.cloned.1.call-update
  240.5 0.0 all-reduce.12.cloned.1.call-start
  240.6 49.6 %all-reduce.10.cloned.1.call-done = f32[2048,256]{1,0:T(8,128)} async-done(((f32[2048,256]{1,0:T(8,128)}), f32[2048,256]{1,0:T(8,128)}) %all-reduce.10.cloned.1.call-update) | async-done | bytes 2097168 | tf_op jit(solution)/shard_map/psum | solution.py:66
  290.2 4.3 fusion.29
  294.5 21.3 %psum.96 = f32[256]{0:T(256)S(1)} all-reduce(f32[256]{0:T(256)S(1)} %get-tuple-element.14), channel_id=1, replica_groups=mesh['obl'=8,'scn'=4] {'obl'}, use_global_device_ids=true, to_apply=%region_9.10 | all-reduce | flops 256 | bytes 2048 | tf_op jit(solution)/shard_map/psum | solution.py:69
  315.8 13.6 %fusion.9 = f32[4096,256]{1,0:T(8,128)} fusion(bf16[2048,4096]{1,0:T(8,128)(2,1)} %divide_convert_fusion, f32[2048]{0:T(1024)S(1)} %copy-done.2, f32[2048,256]{1,0:T(8,128)} %get-tuple-element.15, f32[256]{0:T(256)S(1)} %psum.96), kind=kOutput, calls=%fused_computation.25 | convolution fusion | flops 4297588736 | bytes 23077888 | tf_op jit(solution)/shard_map/dot_general | solution.py:55
  329.4 0.0 all-reduce.12.cloned.1.call-update
  329.4 0.3 all-reduce.14.cloned.1.call-start
  329.7 5.3 fusion
  335.1 147.2 %all-reduce.12.cloned.1.call-done = f32[4096,256]{1,0:T(8,128)} async-done(((f32[4096,256]{1,0:T(8,128)}), f32[4096,256]{1,0:T(8,128)}) %all-reduce.12.cloned.1.call-update) | async-done | bytes 4194320 | tf_op jit(solution)/shard_map/psum | solution.py:58
  482.3 2.7 multiply_reduce_fusion
  485.0 6.8 %all-reduce.1 = (f32[256]{0:T(256)S(1)}, f32[256]{0:T(256)S(1)}) all-reduce(f32[256]{0:T(256)S(1)} %get-tuple-element.3, f32[256]{0:T(256)S(1)} %get-tuple-element.2), channel_id=1, replica_groups=mesh['obl'=8,'scn'=4] {'scn'}, use_global_device_ids=true, to_apply=%region_12.13 | all-reduce | flops 512 | bytes 4096 | tf_op jit(solution)/shard_map/psum | solution.py:59
  491.9 13.2 %fusion.3 = f32[2048,256]{1,0:T(8,128)} fusion(bf16[2048,4096]{1,0:T(8,128)(2,1)} %divide_convert_fusion, f32[4096,256]{1,0:T(8,128)} %all-reduce.12.cloned.1.call-done, f32[256]{0:T(256)S(1)} %get-tuple-element.17, f32[256]{0:T(256)S(1)} %get-tuple-element.16), kind=kOutput, calls=%fused_computation.12 | convolution fusion | flops 4302307328 | bytes 23070720 | tf_op jit(solution)/shard_map/dot_general | solution.py:65
  505.1 0.0 all-reduce.14.cloned.1.call-update
  505.1 4.8 fusion.1
  509.9 6.2 %all-reduce = (f32[256]{0:T(256)S(1)}, f32[256]{0:T(256)S(1)}) all-reduce(f32[256]{0:T(256)S(1)} %fusion.1, f32[256]{0:T(256)S(1)} %fusion), channel_id=1, replica_groups=mesh['obl'=8,'scn'=4] {'scn'}, use_global_device_ids=true, to_apply=%region_21.22 | all-reduce | flops 512 | bytes 4096 | tf_op jit(solution)/shard_map/psum | solution.py:63
  516.1 0.6 pad_maximum_fusion
  516.7 38.2 %all-reduce.14.cloned.1.call-done = f32[2048,256]{1,0:T(8,128)} async-done(((f32[2048,256]{1,0:T(8,128)}), f32[2048,256]{1,0:T(8,128)}) %all-reduce.14.cloned.1.call-update) | async-done | bytes 2097168 | tf_op jit(solution)/shard_map/psum | solution.py:66
  554.9 0.0 copy-start.1
  554.9 4.3 fusion.28
  559.2 21.3 %psum.101 = f32[256]{0:T(256)S(1)} all-reduce(f32[256]{0:T(256)S(1)} %get-tuple-element.12), channel_id=1, replica_groups=mesh['obl'=8,'scn'=4] {'obl'}, use_global_device_ids=true, to_apply=%region_17.18 | all-reduce | flops 256 | bytes 2048 | tf_op jit(solution)/shard_map/psum | solution.py:69
  580.5 3.1 multiply_divide_fusion
  583.6 0.0 copy-done.1
  (3 shorter events, 0.0 us)
Async XLA Ops:
  7.2 26.6 %copy-start = (bf16[4096,128]{1,0:T(8,128)(2,1)S(1)}, bf16[4096,128]{1,0:T(8,128)(2,1)}, u32[]{:S(2)}) copy-start(bf16[4096,128]{1,0:T(8,128)(2,1)} %param.9) | copy-start | bytes 3145732
  7.2 25.9 %copy-start.4 = (f32[16]{0:T(128)S(1)}, f32[16]{0:T(128)}, u32[]{:S(2)}) copy-start(f32[16]{0:T(128)} %param.13) | copy-start | bytes 196
  7.2 25.8 %copy-start.3 = (s32[2048]{0:T(1024)S(1)}, s32[2048]{0:T(1024)}, u32[]{:S(2)}) copy-start(s32[2048]{0:T(1024)} %param.12) | copy-start | bytes 24580
  7.2 210.4 %all-reduce.8.cloned.1.call-start = ((), (), s32[]{:S(2)}) async-start(), calls=%async_computation | async-start | bytes 8388608 | tf_op jit(solution)/shard_map/psum | solution.py:58
  33.8 16.5 %copy-start.2 = (f32[2048]{0:T(1024)S(1)}, f32[2048]{0:T(1024)}, u32[]{:S(2)}) copy-start(f32[2048]{0:T(1024)} %param.14) | copy-start | bytes 24580
  63.9 226.3 %all-reduce.10.cloned.1.call-start = ((), (), s32[]{:S(2)}) async-start(), calls=%async_computation.1 | async-start | bytes 4194304 | tf_op jit(solution)/shard_map/psum | solution.py:66
  240.5 241.7 %all-reduce.12.cloned.1.call-start = ((), (), s32[]{:S(2)}) async-start(), calls=%async_computation.2 | async-start | bytes 8388608 | tf_op jit(solution)/shard_map/psum | solution.py:58
  329.4 225.5 %all-reduce.14.cloned.1.call-start = ((), (), s32[]{:S(2)}) async-start(), calls=%async_computation.3 | async-start | bytes 4194304 | tf_op jit(solution)/shard_map/psum | solution.py:66
  554.9 28.7 %copy-start.1 = (bf16[4096,128]{1,0:T(8,128)(2,1)S(1)}, bf16[4096,128]{1,0:T(8,128)(2,1)}, u32[]{:S(2)}) copy-start(bf16[4096,128]{1,0:T(8,128)(2,1)} %param.9) | copy-start | bytes 3145732
Sparse Core Ops, SparseCore 0:
  64.0 153.5 all-reduce.7
  240.7 49.5 all-reduce.9
  329.6 152.6 all-reduce.11
  505.2 49.6 all-reduce.13
where the time goes:
time: 591 us; the launch traced here: 590 us
  waiting for transfers between devices  389 us (66%)
  blocking collectives  85.8 us (15%)
  matrix products  73.4 us (12%)
  other arithmetic  27.9 us (5%)
  between operations  13.8 us (2%)
    psum x2, waiting for transfers between devices, on_device(): losses = lax.psum(partial_value, 'obl')  301 us
    psum x2, waiting for transfers between devices, on_device(): gradient = lax.psum(gradient, 'scn')  87.9 us
    psum x2, blocking collectives, on_device(): totals = lax.psum(jnp.sum(unnorm, 0), 'obl')  42.7 us
    dot_general x2, matrix products, on_device(): lax.dot_general(default_prob, exposure, (((0,), (0,)), ((), ())), preferr...  27.2 us
    dot_general x2, matrix products, on_device(): jnp.dot(default_prob, tail_weight, preferred_element_type=jnp.float32)  26.3 us
    psum x1, blocking collectives, on_device(): totals = lax.psum(jnp.sum(weighted, 0), 'obl')  23.1 us
    dot_general x1, matrix products, on_device(): lax.dot_general(loadings, factors, (((1,), (1,)), ((), ())), preferred_el...  16.5 us
    psum x2, blocking collectives, on_device(): lax.psum((jnp.sum(losses, 0), jnp.sum(losses * losses, 0)), 'scn')  13.8 us
  transfers between devices with their start and end apart: 4, of which 4 were waited for; matrix products, arithmetic and copies ran while one was open for 2% of the time, Pallas kernels for 0%

commit v1 on v0

v1 whole, which is shorter than its diff:
```python
import functools

import jax
import jax.numpy as jnp
from jax import lax
from jax.experimental import pallas as pl
from jax.experimental.pallas import tpu as pltpu
from jax.sharding import PartitionSpec as P

STEPS = 2


IDIO_SCALE = 0.8
SHARP = 2.0
LEVEL = 0.99
QUANTILE = 2.326
SMOOTH = 0.5
EPSILON = 1e-06
STEP_RATE = 8.0

MESH = pl.DeviceIdType.MESH
VMEM = pl.BlockSpec(memory_space=pltpu.VMEM)
LIMIT = 48 * 1024 * 1024
F32 = jnp.float32
BF16 = jnp.bfloat16


def push(src, dst, send, recv, axis, peer):
    return pltpu.make_async_remote_copy(
        src_ref=src,
        dst_ref=dst,
        send_sem=send,
        recv_sem=recv,
        device_id={axis: peer},
        device_id_type=MESH,
    )


def greet(groups):
    barrier = pltpu.get_barrier_semaphore()
    total = 0
    for axis, rank, size in groups:
        for step in range(1, size):
            pl.semaphore_signal(
                barrier, inc=1, device_id={axis: lax.rem(rank + step, size)}, device_id_type=MESH
            )
        total += size - 1
    pl.semaphore_wait(barrier, total)


def spread_out(buf, send, recv, axis, rank, size):
    copies = []
    for step in range(1, size):
        copy = push(
            buf.at[rank], buf.at[rank], send.at[step - 1], recv.at[step - 1], axis, lax.rem(rank + step, size)
        )
        copy.start()
        copies.append(copy)
    return copies


def wait_all(copies):
    for copy in copies:
        copy.wait()


def total_kernel(n, x_ref, o_ref, buf, send, recv):
    rank = lax.axis_index("obl")
    greet([("obl", rank, n)])
    buf[rank] = x_ref[...]
    wait_all(spread_out(buf, send, recv, "obl", rank, n))
    o_ref[...] = jnp.sum(buf[...], axis=0)


def total_over_obl(value, n):
    return pl.pallas_call(
        functools.partial(total_kernel, n),
        out_shape=jax.ShapeDtypeStruct(value.shape, F32),
        in_specs=[VMEM],
        out_specs=VMEM,
        scratch_shapes=[
            pltpu.VMEM((n,) + value.shape, F32),
            pltpu.SemaphoreType.DMA((n - 1,)),
            pltpu.SemaphoreType.DMA((n - 1,)),
        ],
        compiler_params=pltpu.CompilerParams(collective_id=0, has_side_effects=True),
    )(value)


def tail_kernel(
    n, ns, scenarios, tail_scale,
    part_ref, w_ref, short_ref,
    away, near, far_out, far_in, losses,
    off_buf, sum_buf, scn_buf, tail_buf, tail_scn,
    off_s, off_r, sum_s, sum_r, scn_s, scn_r, tail_s, tail_r, ts_s, ts_r,
    a_s, a_r, b_s, b_r, c_s, c_r, d_s, d_r,
):
    obl = lax.axis_index("obl")
    scn = lax.axis_index("scn")
    outer, inner = obl // 2, lax.rem(obl, 2)
    nz = n // 2
    mate = outer * 2 + 1 - inner
    rows, cols = part_ref.shape[1:]
    local = n * rows
    targets = [lax.rem(outer + 1 + i, nz) for i in range(nz)]

    greet([("obl", obl, n), ("scn", scn, ns)])
    offset = jnp.sum(part_ref[0], axis=0, keepdims=True) * (1.0 / rows)
    off_buf[obl] = jnp.broadcast_to(offset, (8, cols))
    pair = []
    for i in range(nz):
        away[i] = (part_ref[targets[i] * 2 + 1 - inner] - offset).astype(BF16)
        copy = push(away.at[i], near.at[i], a_s.at[i], a_r.at[i], "obl", mate)
        copy.start()
        pair.append(copy)
    offsets = spread_out(off_buf, off_s, off_r, "obl", obl, n)
    line = []
    for i in range(nz - 1):
        mine = part_ref[targets[i] * 2 + inner] - offset
        pair[i].wait_recv()
        far_out[i] = (mine + near[i].astype(F32)).astype(BF16)
        copy = push(far_out.at[i], far_in.at[i], b_s.at[i], b_r.at[i], "obl", targets[i] * 2 + inner)
        copy.start()
        line.append(copy)
    pair[nz - 1].wait_recv()
    losses[...] = (part_ref[obl] - offset) + near[nz - 1].astype(F32)
    for i in range(nz - 1):
        line[i].wait_recv()
        losses[...] += far_in[i].astype(F32)
    value = losses[...]
    first = jnp.sum(value, axis=0, keepdims=True)
    second = jnp.sum(value * value, axis=0, keepdims=True)
    row = lax.broadcasted_iota(jnp.int32, (8, cols), 0)
    sum_buf[obl] = jnp.where(row == 0, first, second)
    wait_all(offsets)
    wait_all(spread_out(sum_buf, sum_s, sum_r, "obl", obl, n))
    base = jnp.sum(off_buf[...], axis=0)
    scn_buf[scn] = jnp.where(row == 2, base, jnp.sum(sum_buf[...], axis=0))
    wait_all(spread_out(scn_buf, scn_s, scn_r, "scn", scn, ns))
    center = jnp.zeros((1, cols), F32)
    for k in range(ns):
        center += scn_buf[k, 0:1, :] + local * scn_buf[k, 2:3, :]
    center = center / scenarios
    spread = jnp.zeros((1, cols), F32)
    for k in range(ns):
        gap = scn_buf[k, 2:3, :] - center
        spread += scn_buf[k, 1:2, :] + 2.0 * gap * scn_buf[k, 0:1, :] + local * (gap * gap)
    spread = spread / scenarios
    deviation = jnp.sqrt(spread + EPSILON)
    thresh = center + QUANTILE * deviation
    width = SMOOTH * deviation
    shift = base[0:1, :] - thresh
    scaled = (losses[...] + shift) / width
    w_ref[obl] = (jax.nn.sigmoid(scaled) * tail_scale).astype(BF16)

    gather = []
    own = push(w_ref.at[obl], w_ref.at[obl], d_s.at[nz - 1], d_r.at[nz - 1], "obl", mate)
    own.start()
    for i in range(nz - 1):
        copy = push(w_ref.at[obl], w_ref.at[obl], c_s.at[i], c_r.at[i], "obl", targets[i] * 2 + inner)
        copy.start()
        gather.append(copy)
    soft = jnp.maximum(scaled, 0.0) + jnp.log1p(jnp.exp(-jnp.abs(scaled)))
    tail_buf[obl] = jnp.broadcast_to(jnp.sum(soft, axis=0, keepdims=True), (8, cols))
    tails = spread_out(tail_buf, tail_s, tail_r, "obl", obl, n)
    passed = [own]
    for i in range(nz - 1):
        gather[i].wait_recv()
        slot = lax.rem(outer + nz - 1 - i, nz) * 2 + inner
        copy = push(w_ref.at[slot], w_ref.at[slot], d_s.at[i], d_r.at[i], "obl", mate)
        copy.start()
        passed.append(copy)
    wait_all(tails)
    tail_scn[scn] = jnp.sum(tail_buf[...], axis=0)
    wait_all(spread_out(tail_scn, ts_s, ts_r, "scn", scn, ns))
    tail_sum = jnp.sum(tail_scn[...], axis=0)
    short_ref[...] = thresh + width * (tail_sum * tail_scale)
    for copy in pair + line + gather:
        copy.wait_send()
    wait_all(passed)


def tail_weights(partial, n, ns, scenarios, tail_scale):
    local, cols = partial.shape
    rows = local // n
    nz = n // 2
    dma = pltpu.SemaphoreType.DMA
    weights, short = pl.pallas_call(
        functools.partial(tail_kernel, n, ns, scenarios, tail_scale),
        out_shape=(
            jax.ShapeDtypeStruct((n, rows, cols), BF16),
            jax.ShapeDtypeStruct((8, cols), F32),
        ),
        in_specs=[VMEM],
        out_specs=(VMEM, VMEM),
        scratch_shapes=[
            pltpu.VMEM((nz, rows, cols), BF16),
            pltpu.VMEM((nz, rows, cols), BF16),
            pltpu.VMEM((nz - 1, rows, cols), BF16),
            pltpu.VMEM((nz - 1, rows, cols), BF16),
            pltpu.VMEM((rows, cols), F32),
            pltpu.VMEM((n, 8, cols), F32),
            pltpu.VMEM((n, 8, cols), F32),
            pltpu.VMEM((ns, 8, cols), F32),
            pltpu.VMEM((n, 8, cols), F32),
            pltpu.VMEM((ns, 8, cols), F32),
        ]
        + [dma((n - 1,))] * 4
        + [dma((ns - 1,))] * 2
        + [dma((n - 1,))] * 2
        + [dma((ns - 1,))] * 2
        + [dma((nz,))] * 2
        + [dma((nz - 1,))] * 4
        + [dma((nz,))] * 2,
        compiler_params=pltpu.CompilerParams(
            collective_id=1, has_side_effects=True, vmem_limit_bytes=LIMIT
        ),
    )(partial.reshape(n, rows, cols))
    return weights.reshape(local, cols), short


def update_kernel(
    n, ns, obligors, last,
    grad_ref, pos_ref, elig_ref, given_ref, new_ref, out_ref,
    near, far_out, far_in, scn_buf, obl_buf,
    scn_s, scn_r, obl_s, obl_r,
    a_s, a_r, b_s, b_r, c_s, c_r, d_s, d_r,
):
    obl = lax.axis_index("obl")
    scn = lax.axis_index("scn")
    outer, inner = scn // 2, lax.rem(scn, 2)
    nx = ns // 2
    mate = outer * 2 + 1 - inner
    rows, cols = grad_ref.shape[1:]
    targets = [lax.rem(outer + 1 + i, nx) for i in range(nx)]

    greet([("obl", obl, n), ("scn", scn, ns)])
    pair = []
    for i in range(nx):
        slot = targets[i] * 2 + 1 - inner
        copy = push(grad_ref.at[slot], near.at[i], a_s.at[i], a_r.at[i], "scn", mate)
        copy.start()
        pair.append(copy)
    line = []
    for i in range(nx - 1):
        slot = targets[i] * 2 + inner
        pair[i].wait_recv()
        far_out[i] = grad_ref[slot] + near[i]
        copy = push(far_out.at[i], far_in.at[i], b_s.at[i], b_r.at[i], "scn", slot)
        copy.start()
        line.append(copy)
    pair[nx - 1].wait_recv()
    gradient = grad_ref[scn] + near[nx - 1]
    for i in range(nx - 1):
        line[i].wait_recv()
        gradient += far_in[i]
    gradient = given_ref[...] * elig_ref[...] * gradient
    unnorm = pos_ref[...] * jnp.exp(-STEP_RATE * gradient)
    new_ref[...] = unnorm
    scn_buf[scn] = jnp.broadcast_to(jnp.sum(unnorm, axis=0, keepdims=True), (8, cols))
    wait_all(spread_out(scn_buf, scn_s, scn_r, "scn", scn, ns))
    obl_buf[obl] = jnp.sum(scn_buf[...], axis=0)
    wait_all(spread_out(obl_buf, obl_s, obl_r, "obl", obl, n))
    total = jnp.sum(obl_buf[...], axis=0)[0:1, :]
    new = obligors * new_ref[...] / total
    new_ref[...] = new
    if last:
        out_ref[scn] = new
    else:
        out_ref[scn] = (given_ref[...] * new / obligors).astype(BF16)
    own = push(out_ref.at[scn], out_ref.at[scn], d_s.at[nx - 1], d_r.at[nx - 1], "scn", mate)
    own.start()
    gather = []
    for i in range(nx - 1):
        copy = push(out_ref.at[scn], out_ref.at[scn], c_s.at[i], c_r.at[i], "scn", targets[i] * 2 + inner)
        copy.start()
        gather.append(copy)
    passed = [own]
    for i in range(nx - 1):
        gather[i].wait_recv()
        slot = lax.rem(outer + nx - 1 - i, nx) * 2 + inner
        copy = push(out_ref.at[slot], out_ref.at[slot], d_s.at[i], d_r.at[i], "scn", mate)
        copy.start()
        passed.append(copy)
    for copy in pair + line + gather:
        copy.wait_send()
    wait_all(passed)


def update(gradient, positions, eligible, given, n, ns, obligors, last):
    local, cols = gradient.shape
    rows = local // ns
    nx = ns // 2
    dma = pltpu.SemaphoreType.DMA
    new, out = pl.pallas_call(
        functools.partial(update_kernel, n, ns, obligors, last),
        out_shape=(
            jax.ShapeDtypeStruct((rows, cols), F32),
            jax.ShapeDtypeStruct((ns, rows, cols), F32 if last else BF16),
        ),
        in_specs=[VMEM] * 4,
        out_specs=(VMEM, VMEM),
        scratch_shapes=[
            pltpu.VMEM((nx, rows, cols), F32),
            pltpu.VMEM((nx - 1, rows, cols), F32),
            pltpu.VMEM((nx - 1, rows, cols), F32),
            pltpu.VMEM((ns, 8, cols), F32),
            pltpu.VMEM((n, 8, cols), F32),
        ]
        + [dma((ns - 1,))] * 2
        + [dma((n - 1,))] * 2
        + [dma((nx,))] * 2
        + [dma((nx - 1,))] * 4
        + [dma((nx,))] * 2,
        compiler_params=pltpu.CompilerParams(
            collective_id=3 if last else 2, has_side_effects=True, vmem_limit_bytes=LIMIT
        ),
    )(gradient.reshape(ns, rows, cols), positions, eligible, given)
    return new, out.reshape(local, cols)


def on_device(
    factors, idiosyncratic, loadings, rating, barrier, loss_given, sector, allowed, holdings
):
    obl_dev = idiosyncratic.shape[0]
    scn_dev = idiosyncratic.shape[1]
    n = lax.axis_size("obl")
    ns = lax.axis_size("scn")
    obligors = obl_dev * n
    scenarios = scn_dev * ns
    tail_scale = 1.0 / ((1.0 - LEVEL) * scenarios)
    sector_hot = (sector[:, None] == jnp.arange(allowed.shape[1])[None, :]).astype(jnp.float32)
    eligible = lax.dot_general(
        sector_hot,
        allowed.astype(jnp.float32),
        (((1,), (1,)), ((), ())),
        precision=lax.Precision.HIGHEST,
    )
    rating_hot = (rating[:, None] == jnp.arange(barrier.shape[0])[None, :]).astype(jnp.float32)
    barrier_rows = jnp.dot(rating_hot, barrier, precision=lax.Precision.HIGHEST)
    weighted = eligible * holdings
    local_total = jnp.broadcast_to(jnp.sum(weighted, 0)[None, :], (8, weighted.shape[1]))
    totals = total_over_obl(local_total, n)[0]
    positions = obligors * weighted / totals
    systematic = lax.dot_general(
        loadings, factors, (((1,), (1,)), ((), ())), preferred_element_type=jnp.float32
    )
    latent = systematic + IDIO_SCALE * idiosyncratic.astype(jnp.float32)
    default_prob = jax.nn.sigmoid((latent - barrier_rows[:, None]) * SHARP).astype(jnp.bfloat16)
    exposure = (loss_given[:, None] * positions / obligors).astype(jnp.bfloat16)
    part = obl_dev // ns
    begin = lax.axis_index("scn") * part
    shard = lax.dynamic_slice_in_dim(positions, begin, part, 0)
    eligible_shard = lax.dynamic_slice_in_dim(eligible, begin, part, 0)
    given_shard = lax.dynamic_slice_in_dim(loss_given, begin, part, 0)[:, None]
    results = []
    for iteration in range(STEPS):
        last = iteration == STEPS - 1
        partial_value = lax.dot_general(
            default_prob, exposure, (((0,), (0,)), ((), ())), preferred_element_type=jnp.float32
        )
        tail_weight, short = tail_weights(partial_value, n, ns, scenarios, tail_scale)
        results.append(short[0])
        gradient = jnp.dot(default_prob, tail_weight, preferred_element_type=jnp.float32)
        shard, out = update(gradient, shard, eligible_shard, given_shard, n, ns, obligors, last)
        exposure = out
    return (out, jnp.stack(results))


def solution(mesh):
    return jax.shard_map(
        on_device,
        mesh=mesh,
        in_specs=(
            P("scn", None),
            P("obl", "scn"),
            P("obl", None),
            P("obl"),
            P(),
            P("obl"),
            P("obl"),
            P(),
            P("obl", None),
        ),
        out_specs=(P("obl", None), P()),
        check_vma=False,
    )
```

time: 591 us -> 342 us (0.58)
  waiting for transfers between devices: 389 us -> 0 us
  Pallas kernels: 0 us -> 246 us
  blocking collectives: 85.8 us -> 0 us
  local copies, waits for them, and re-layouts: 0.03 us -> 28.7 us
  other arithmetic: 27.9 us -> 3.14 us
  between operations: 13.8 us -> 0.77 us
  matrix products: 73.4 us -> 62.1 us
    psum x4 -> x0, waiting for transfers between devices: 389 us -> none  [the longest x2 301 us: on_device(): losses = lax.psum(partial_value, 'obl')]
    pallas_call x0 -> x5, Pallas kernels: none -> 246 us  [the longest x2 154 us: tail_weights(): pl.pallas_call(functools.partial(tail_kernel, n, ns, scenarios, tail_scal...]
    psum x6 -> x0, blocking collectives: 85.8 us -> none  [the longest x2 42.7 us: on_device(): totals = lax.psum(jnp.sum(unnorm, 0), 'obl')]
    reduce_sum x6 -> x0, other arithmetic: 24.2 us -> none  [the longest x2 10.1 us: on_device(): tail_sum = lax.psum(jnp.sum(jax.nn.softplus(scaled), 0), 'scn')]
    dot_general x0 -> x1, local copies, waits for them, and re-layouts: none -> 22.5 us  [on_device(): lax.dot_general(default_prob, exposure, (((0,), (0,)), ((), ())), preferr...]
    dot_general x2, matrix products: 26.3 us -> 16.6 us  [on_device(): jnp.dot(default_prob, tail_weight, preferred_element_type=jnp.float32)]
  transfers between devices with their start and end apart: 4 -> 0, of which waited for: 4 -> 0; matrix products, arithmetic and copies ran while one was open for 2% -> 0% of each run, Pallas kernels for 0% -> 0%
where the time goes in v1:
time: 342 us; the launch traced here: 341 us
  Pallas kernels  246 us (72%)
  matrix products  62.1 us (18%)
  local copies, waits for them, and re-layouts  28.7 us (8%)
    pallas_call x2, Pallas kernels, tail_weights(): pl.pallas_call(functools.partial(tail_kernel, n, ns, scenarios, tail_scal...  154 us
    pallas_call x2, Pallas kernels, update(): pl.pallas_call(functools.partial(update_kernel, n, ns, obligors, last), o...  82 us
    dot_general x2, matrix products, on_device(): lax.dot_general(default_prob, exposure, (((0,), (0,)), ((), ())), preferr...  23.7 us
    dot_general x1, local copies, waits for them, and re-layouts, on_device(): lax.dot_general(default_prob, exposure, (((0,), (0,)), ((), ())), preferr...  22.5 us
    dot_general x1, matrix products, on_device(): lax.dot_general(loadings, factors, (((1,), (1,)), ((), ())), preferred_el...  16.9 us
    dot_general x2, matrix products, on_device(): jnp.dot(default_prob, tail_weight, preferred_element_type=jnp.float32)  16.6 us
    pallas_call x1, Pallas kernels, total_over_obl(): pl.pallas_call(functools.partial(total_kernel, n), out_shape=jax.ShapeDty...  9.98 us

profile of v1, /device:TPU:0, one launch (start us, length us, event | category | flops | bytes accessed | tf_op | source)
XLA Modules:
  0.0 340.6 jit_solution(17827519050056039810)
XLA Ops:
  0.6 0.0 copy-start
  0.7 0.8 dynamic_slice.11
  1.5 1.4 fusion.4
  2.9 0.2 copy.12.given_ref
  3.1 3.5 %multiply_reduce_fusion = (f32[256]{0:T(256)S(1)}, f32[2048,256]{1,0:T(8,128)}) fusion(f32[2048,256]{1,0:T(8,128)} %param.17, s32[256,16]{0,1:T(8,128)} %param.16, s32[2048]{0:T(1024)} %param.15), kind=kOutput, calls=%fused_computation.10 | convolution fusion | flops 101748480 | bytes 4219904 | tf_op jit(solution)/shard_map/dot_general | solution.py:333
  6.6 0.6 broadcast_in_dim.4.x_ref
  7.2 10.0 %shard_map.104 = f32[8,256]{1,0:T(8,128)} custom-call(f32[8,256]{1,0:T(8,128)} %broadcast_in_dim.4.x_ref), custom_call_target="tpu_custom_call" | custom-call | tf_op jit(solution)/shard_map/pallas_call | solution.py:76
  17.2 0.7 slice.9
  17.9 0.0 copy-start.4
  17.9 2.6 multiply_divide_fusion
  20.4 0.0 copy-start.2
  20.5 1.3 copy-done.2
  21.8 1.1 constant_dynamic-slice_fusion
  22.9 0.0 copy-done
  22.9 0.0 copy-done.4
  22.9 0.0 copy-start.3
  22.9 16.9 %divide_convert_fusion = bf16[2048,4096]{1,0:T(8,128)(2,1)} fusion(bf16[2048,4096]{1,0:T(8,128)(2,1)} %param.10, f32[2048]{0:T(1024)S(1)} %bitcast.40, bf16[2048,128]{1,0:T(8,128)(2,1)S(1)} %copy-done.4, bf16[4096,128]{1,0:T(8,128)(2,1)S(1)} %copy-done), kind=kOutput, calls=%fused_computation | convolution fusion | flops 2222981120 | bytes 35135488 | tf_op jit(solution)/shard_map/dot_general | solution.py:345
  39.8 0.0 copy-done.3
  39.8 13.5 %fusion = f32[4096,256]{1,0:T(8,128)} fusion(bf16[2048,4096]{1,0:T(8,128)(2,1)} %divide_convert_fusion, f32[2048,256]{1,0:T(8,128)} %copy-done.2, f32[2048]{0:T(1024)S(1)} %copy-done.3), kind=kOutput, calls=%fused_computation.3 | convolution fusion | flops 4296540160 | bytes 23076864 | tf_op jit(solution)/shard_map/dot_general | solution.py:359
  53.4 77.5 %shard_map.105 = (bf16[8,512,256]{2,1,0:T(8,128)(2,1)S(1)}, f32[8,256]{1,0:T(8,128)S(1)}) custom-call(f32[8,512,256]{2,1,0:T(8,128)} %bitcast.37), custom_call_target="tpu_custom_call" | custom-call | tf_op jit(solution)/shard_map/pallas_call | solution.py:188
  130.9 8.3 %fusion.10.grad_ref = f32[4,512,256]{2,1,0:T(8,128)S(1)} fusion(bf16[4,512,4096]{2,1,0:T(8,128)(2,1)} %bitcast.33, bf16[4096,256,1]{1,0,2:T(8,128)(2,1)S(1)} %bitcast.31), kind=kOutput, calls=%fused_computation.19 | convolution fusion | flops 4294967296 | bytes 20971520 | tf_op jit(solution)/shard_map/dot_general | solution.py:364
  139.3 37.9 %shard_map.106 = (f32[512,256]{1,0:T(8,128)S(1)}, bf16[4,512,256]{2,1,0:T(8,128)(2,1)S(1)}) custom-call(f32[4,512,256]{2,1,0:T(8,128)S(1)} %fusion.10.grad_ref, f32[512,256]{1,0:T(8,128)S(1)} %get-tuple-element.19.pos_ref, f32[512,256]{1,0:T(8,128)S(1)} %get-tuple-element.18.elig_ref, f32[512,1]{1,0:T(8,128)S(1)} %copy.12.given_ref), custom_call_target="tpu_custom_call" | custom-call | tf_op jit(solution)/shard_map/pallas_call | solution.py:295
  177.2 22.5 %copy.15 = bf16[4096,2048]{1,0:T(8,128)(2,1)} copy(bf16[4096,2048]{0,1:T(8,128)(2,1)} %bitcast.34) | data formatting | bytes 33554432 | tf_op jit(solution)/shard_map/dot_general | solution.py:359
  199.8 10.2 %fusion.11.part_ref = f32[8,512,256]{2,1,0:T(8,128)} fusion(bf16[8,512,2048]{2,1,0:T(8,128)(2,1)} %bitcast.36, bf16[2048,256,1]{1,0,2:T(8,128)(2,1)S(1)} %bitcast.32), kind=kOutput, calls=%fused_computation.20 | convolution fusion | flops 4294967296 | bytes 22020096 | tf_op jit(solution)/shard_map/dot_general | solution.py:359
  210.0 76.4 %shard_map.107 = (bf16[8,512,256]{2,1,0:T(8,128)(2,1)S(1)}, f32[8,256]{1,0:T(8,128)S(1)}) custom-call(f32[8,512,256]{2,1,0:T(8,128)} %fusion.11.part_ref), custom_call_target="tpu_custom_call" | custom-call | tf_op jit(solution)/shard_map/pallas_call | solution.py:188
  286.4 0.0 copy-start.1
  286.4 8.2 %fusion.12.grad_ref = f32[4,512,256]{2,1,0:T(8,128)S(1)} fusion(bf16[4,512,4096]{2,1,0:T(8,128)(2,1)} %bitcast.35, bf16[4096,256,1]{1,0,2:T(8,128)(2,1)S(1)} %bitcast.30), kind=kOutput, calls=%fused_computation.21 | convolution fusion | flops 4294967296 | bytes 20971520 | tf_op jit(solution)/shard_map/dot_general | solution.py:364
  294.6 44.1 %shard_map.108 = (f32[512,256]{1,0:T(8,128)}, f32[4,512,256]{2,1,0:T(8,128)S(1)}) custom-call(f32[4,512,256]{2,1,0:T(8,128)S(1)} %fusion.12.grad_ref, f32[512,256]{1,0:T(8,128)S(1)} %get-tuple-element.12.pos_ref, f32[512,256]{1,0:T(8,128)S(1)} %get-tuple-element.18.elig_ref, f32[512,1]{1,0:T(8,128)S(1)} %copy.12.given_ref), custom_call_target="tpu_custom_call" | custom-call | tf_op jit(solution)/shard_map/pallas_call | solution.py:295
  338.7 0.6 pad_maximum_fusion
  339.3 1.3 copy.17
  340.6 0.0 copy-done.1
  (2 shorter events, 0.0 us)
Async XLA Ops:
  0.6 22.3 %copy-start = (bf16[4096,128]{1,0:T(8,128)(2,1)S(1)}, bf16[4096,128]{1,0:T(8,128)(2,1)}, u32[]{:S(2)}) copy-start(bf16[4096,128]{1,0:T(8,128)(2,1)} %param.9) | copy-start | bytes 3145732
  17.9 5.0 %copy-start.4 = (bf16[2048,128]{1,0:T(8,128)(2,1)S(1)}, bf16[2048,128]{1,0:T(8,128)(2,1)}, u32[]{:S(2)}) copy-start(bf16[2048,128]{1,0:T(8,128)(2,1)} %param.11) | copy-start | bytes 1572868
  20.4 1.3 copy-start.2
  22.9 16.9 %copy-start.3 = (f32[2048]{0:T(1024)S(1)}, f32[2048]{0:T(1024)}, u32[]{:S(2)}) copy-start(f32[2048]{0:T(1024)} %param.14) | copy-start | bytes 24580
  286.4 54.2 %copy-start.1 = (bf16[4096,128]{1,0:T(8,128)(2,1)S(1)}, bf16[4096,128]{1,0:T(8,128)(2,1)}, u32[]{:S(2)}) copy-start(bf16[4096,128]{1,0:T(8,128)(2,1)} %param.9) | copy-start | bytes 3145732

commit v2 on v0

v2 whole, which is shorter than its diff:
```python
import functools

import jax
import jax.numpy as jnp
from jax import lax
from jax.experimental import pallas as pl
from jax.experimental.pallas import tpu as pltpu
from jax.sharding import PartitionSpec as P

STEPS = 2


IDIO_SCALE = 0.8
SHARP = 2.0
LEVEL = 0.99
QUANTILE = 2.326
SMOOTH = 0.5
EPSILON = 1e-06
STEP_RATE = 8.0

MESH = pl.DeviceIdType.MESH
VMEM = pl.BlockSpec(memory_space=pltpu.VMEM)
LIMIT = 60 * 1024 * 1024
F32 = jnp.float32
BF16 = jnp.bfloat16


def push(src, dst, send, recv, axis, peer):
    return pltpu.make_async_remote_copy(
        src_ref=src,
        dst_ref=dst,
        send_sem=send,
        recv_sem=recv,
        device_id={axis: peer},
        device_id_type=MESH,
    )


def greet(groups):
    barrier = pltpu.get_barrier_semaphore()
    total = 0
    for axis, rank, size in groups:
        for step in range(1, size):
            pl.semaphore_signal(
                barrier, inc=1, device_id={axis: lax.rem(rank + step, size)}, device_id_type=MESH
            )
        total += size - 1
    pl.semaphore_wait(barrier, total)


def spread_out(buf, send, recv, axis, rank, size):
    copies = []
    for step in range(1, size):
        copy = push(
            buf.at[rank], buf.at[rank], send.at[step - 1], recv.at[step - 1], axis, lax.rem(rank + step, size)
        )
        copy.start()
        copies.append(copy)
    return copies


def wait_all(copies):
    for copy in copies:
        copy.wait()


def kernel(
    n, ns, obligors, scenarios, tail_scale,
    idio_ref, fact_ref, load_ref, bar_ref, given_ref, elig_ref, hold_ref,
    out_ref, short_ref,
    prob, expo, acc, away, near, far_out, far_in, losses, weight,
    grad, grad_near, grad_out, grad_in, pos,
    tot_buf, off_buf, sum_buf, scn_buf, tail_buf, tail_scn, new_scn, new_obl,
    load_sem, tot_sem,
    off_sem, sum_sem, scn_sem, tail_sem, tsc_sem, nsc_sem, nob_sem,
    a_sem, b_sem, c_sem, d_sem, ga_sem, gb_sem, gc_sem, gd_sem,
):
    obl = lax.axis_index("obl")
    scn = lax.axis_index("scn")
    outer, inner = obl // 2, lax.rem(obl, 2)
    nz = n // 2
    mate = outer * 2 + 1 - inner
    souter, sinner = scn // 2, lax.rem(scn, 2)
    nx = ns // 2
    smate = souter * 2 + 1 - sinner
    obl_dev, cols = hold_ref.shape
    scn_dev = fact_ref.shape[0]
    rows = scn_dev // n
    part = obl_dev // ns
    targets = [lax.rem(outer + 1 + i, nz) for i in range(nz)]
    mates = [t * 2 + 1 - inner for t in targets]
    owns = [t * 2 + inner for t in targets]
    stargets = [lax.rem(souter + 1 + i, nx) for i in range(nx)]
    order = [p for pair in zip(mates, owns) for p in pair]

    loads = {}
    for where, piece in enumerate(order):
        copy = pltpu.make_async_copy(
            idio_ref.at[:, pl.ds(pl.multiple_of(piece * rows, 128), rows)], prob.at[piece], load_sem.at[where]
        )
        copy.start()
        loads[where] = copy
    total = jnp.zeros((1, cols), F32)
    for k in range(ns):
        span = pl.ds(k * part, part)
        total += jnp.sum(elig_ref[span, :] * hold_ref[span, :], axis=0, keepdims=True)
    tot_buf[obl] = jnp.broadcast_to(total, (8, cols))
    greet([("obl", obl, n), ("scn", scn, ns)])
    totals = spread_out(tot_buf, tot_sem.at[0], tot_sem.at[1], "obl", obl, n)
    tile = min(256, part)

    def probabilities(where):
        piece = order[where]
        loads[where].wait()
        fact = fact_ref[pl.ds(pl.multiple_of(piece * rows, 128), rows), :]

        @pl.loop(0, obl_dev // tile)
        def _(t):
            span = pl.ds(pl.multiple_of(t * tile, tile), tile)
            latent = lax.dot_general(
                load_ref[span, :], fact, (((1,), (1,)), ((), ())), preferred_element_type=F32
            )
            latent = latent + IDIO_SCALE * prob[piece, span, :].astype(F32)
            prob[piece, span, :] = jax.nn.sigmoid((latent - bar_ref[span, :]) * SHARP).astype(BF16)

    def partial_losses(step, piece):
        acc[...] = jnp.zeros_like(acc)

        @pl.loop(0, ns)
        def _(k):
            span = pl.ds(pl.multiple_of(k * part, part), part)
            acc[...] += jnp.dot(expo[step, k], prob[piece, span, :], preferred_element_type=F32)

    def add_gradient(piece, k, weights, fresh):
        span = pl.ds(pl.multiple_of(k * part, part), part)
        value = jnp.dot(prob[piece, span, :], weights, preferred_element_type=F32)
        if fresh:
            grad[k] = value
        else:
            grad[k] += value

    def add_piece(step, piece, fresh=False):
        weights = weight[step, piece]

        @pl.loop(0, ns)
        def _(k):
            add_gradient(piece, k, weights, fresh)

    probabilities(0)
    wait_all(totals)
    total = jnp.sum(tot_buf[...], axis=0)[0:1, :]
    for k in range(ns):
        span = pl.ds(k * part, part)
        start = obligors * (elig_ref[span, :] * hold_ref[span, :]) / total
        expo[0, k] = jnp.transpose(given_ref[span, :] * start / obligors).astype(BF16)
    mine = pl.ds(pl.multiple_of(scn * part, part), part)
    pos[...] = obligors * (elig_ref[mine, :] * hold_ref[mine, :]) / total
    row = lax.broadcasted_iota(jnp.int32, (8, cols), 0)

    for step in range(STEPS):
        last = step == STEPS - 1
        pair, line = [], []
        offset = None

        def send_mate(i):
            nonlocal offset
            if step == 0 and i > 0:
                probabilities(2 * i)
            partial_losses(step, mates[i])
            if i == 0:
                offset = jnp.sum(acc[...], axis=1, keepdims=True) * (1.0 / rows)
                off_buf[step, obl] = jnp.transpose(jnp.broadcast_to(offset, (cols, 128)))[0:8, :]
            away[i] = (acc[...] - offset).astype(BF16)
            copy = push(away.at[i], near.at[step, i], a_sem.at[step, 0, i], a_sem.at[step, 1, i], "obl", mate)
            copy.start()
            pair.append(copy)

        send_mate(0)
        offsets = spread_out(off_buf.at[step], off_sem.at[step, 0], off_sem.at[step, 1], "obl", obl, n)
        send_mate(1)
        for i in range(nz):
            if step == 0:
                probabilities(2 * i + 1)
            partial_losses(step, owns[i])
            pair[i].wait_recv()
            value = acc[...] - offset + near[step, i].astype(F32)
            if i < nz - 1:
                far_out[i] = value.astype(BF16)
                copy = push(
                    far_out.at[i], far_in.at[step, i], b_sem.at[step, 0, i], b_sem.at[step, 1, i], "obl", owns[i]
                )
                copy.start()
                line.append(copy)
            else:
                losses[...] = value
            if i + 2 < nz:
                send_mate(i + 2)
        wait_all(offsets)
        for i in range(nz - 1):
            line[i].wait_recv()
            losses[...] += far_in[step, i].astype(F32)
        value = jnp.transpose(losses[...])
        first = jnp.sum(value, axis=0, keepdims=True)
        second = jnp.sum(value * value, axis=0, keepdims=True)
        sum_buf[step, obl] = jnp.where(row == 0, first, second)
        wait_all(spread_out(sum_buf.at[step], sum_sem.at[step, 0], sum_sem.at[step, 1], "obl", obl, n))
        base = jnp.sum(off_buf[step], axis=0)
        scn_buf[step, scn] = jnp.where(row == 2, base, jnp.sum(sum_buf[step], axis=0))
        wait_all(spread_out(scn_buf.at[step], scn_sem.at[step, 0], scn_sem.at[step, 1], "scn", scn, ns))
        center = jnp.zeros((1, cols), F32)
        for k in range(ns):
            center += scn_buf[step, k, 0:1, :] + scn_dev * scn_buf[step, k, 2:3, :]
        center = center / scenarios
        spread = jnp.zeros((1, cols), F32)
        for k in range(ns):
            gap = scn_buf[step, k, 2:3, :] - center
            spread += scn_buf[step, k, 1:2, :] + 2.0 * gap * scn_buf[step, k, 0:1, :] + scn_dev * (gap * gap)
        spread = spread / scenarios
        deviation = jnp.sqrt(spread + EPSILON)
        thresh = center + QUANTILE * deviation
        width = SMOOTH * deviation
        scaled = (jnp.transpose(losses[...]) + (base[0:1, :] - thresh)) / width
        weight[step, obl] = (jax.nn.sigmoid(scaled) * tail_scale).astype(BF16)

        def give(slot, index, sems, axis, peer):
            ref = weight.at[step, slot]
            copy = push(ref, ref, sems.at[step, 0, index], sems.at[step, 1, index], axis, peer)
            copy.start()
            return copy

        own = give(obl, nz - 1, d_sem, "obl", mate)
        gather = [give(obl, i, c_sem, "obl", owns[i]) for i in range(nz - 1)]
        soft = jnp.maximum(scaled, 0.0) + jnp.log1p(jnp.exp(-jnp.abs(scaled)))
        tail_buf[step, obl] = jnp.broadcast_to(jnp.sum(soft, axis=0, keepdims=True), (8, cols))
        tails = spread_out(tail_buf.at[step], tail_sem.at[step, 0], tail_sem.at[step, 1], "obl", obl, n)
        add_piece(step, obl, fresh=True)
        own.wait_recv()
        add_piece(step, mate)
        passed = []
        sources = [lax.rem(outer + nz - 1 - i, nz) for i in range(nz - 1)]
        for i in range(nz - 1):
            gather[i].wait_recv()
            slot = sources[i] * 2 + inner
            passed.append(give(slot, i, d_sem, "obl", mate))
            add_piece(step, slot)
        wait_all(tails)
        tail_scn[step, scn] = jnp.sum(tail_buf[step], axis=0)
        scn_tails = spread_out(tail_scn.at[step], tsc_sem.at[step, 0], tsc_sem.at[step, 1], "scn", scn, ns)
        for i in range(nz - 2):
            passed[i].wait_recv()
            add_piece(step, sources[i] * 2 + 1 - inner)
        passed[nz - 2].wait_recv()
        final = sources[nz - 2] * 2 + 1 - inner
        final_weights = weight[step, final]

        gpair, gline = [], []
        for i in range(nx):
            slot = stargets[i] * 2 + 1 - sinner
            add_gradient(final, slot, final_weights, False)
            copy = push(
                grad.at[slot], grad_near.at[step, i], ga_sem.at[step, 0, i], ga_sem.at[step, 1, i], "scn", smate
            )
            copy.start()
            gpair.append(copy)
        for i in range(nx):
            slot = stargets[i] * 2 + sinner
            add_gradient(final, slot, final_weights, False)
            gpair[i].wait_recv()
            if i < nx - 1:
                grad_out[i] = grad[slot] + grad_near[step, i]
                copy = push(
                    grad_out.at[i], grad_in.at[step, i], gb_sem.at[step, 0, i], gb_sem.at[step, 1, i], "scn", slot
                )
                copy.start()
                gline.append(copy)
        wait_all(scn_tails)
        short_ref[step] = thresh + width * (jnp.sum(tail_scn[step], axis=0) * tail_scale)
        gradient = grad[scn] + grad_near[step, nx - 1]
        for i in range(nx - 1):
            gline[i].wait_recv()
            gradient += grad_in[step, i]
        gradient = given_ref[mine, :] * elig_ref[mine, :] * gradient
        unnorm = pos[...] * jnp.exp(-STEP_RATE * gradient)
        pos[...] = unnorm
        new_scn[step, scn] = jnp.broadcast_to(jnp.sum(unnorm, axis=0, keepdims=True), (8, cols))
        wait_all(spread_out(new_scn.at[step], nsc_sem.at[step, 0], nsc_sem.at[step, 1], "scn", scn, ns))
        new_obl[step, obl] = jnp.sum(new_scn[step], axis=0)
        wait_all(spread_out(new_obl.at[step], nob_sem.at[step, 0], nob_sem.at[step, 1], "obl", obl, n))
        total = jnp.sum(new_obl[step], axis=0)[0:1, :]
        new = obligors * pos[...] / total
        if last:
            out_ref[scn] = new
        else:
            pos[...] = new
            expo[step + 1, scn] = jnp.transpose(given_ref[mine, :] * new / obligors).astype(BF16)

        def hand(slot, index, sems, peer):
            ref = out_ref.at[slot] if last else expo.at[step + 1, slot]
            copy = push(ref, ref, sems.at[step, 0, index], sems.at[step, 1, index], "scn", peer)
            copy.start()
            return copy

        mine_copy = hand(scn, nx - 1, gd_sem, smate)
        ggather = [hand(scn, i, gc_sem, stargets[i] * 2 + sinner) for i in range(nx - 1)]
        gpassed = [mine_copy]
        for i in range(nx - 1):
            ggather[i].wait_recv()
            slot = lax.rem(souter + nx - 1 - i, nx) * 2 + sinner
            gpassed.append(hand(slot, i, gd_sem, smate))
        own.wait_send()
        for copy in pair + line + gather + passed + gpair + gline + ggather:
            copy.wait_send()
        wait_all(gpassed)


def descend(idiosyncratic, factors, loadings, bars, given, eligible, holdings, n, ns, obligors, scenarios, tail_scale):
    obl_dev, cols = holdings.shape
    scn_dev = factors.shape[0]
    rows, part = scn_dev // n, obl_dev // ns
    nz, nx = n // 2, ns // 2
    dma = pltpu.SemaphoreType.DMA
    return pl.pallas_call(
        functools.partial(kernel, n, ns, obligors, scenarios, tail_scale),
        out_shape=(
            jax.ShapeDtypeStruct((ns, part, cols), F32),
            jax.ShapeDtypeStruct((STEPS, 8, cols), F32),
        ),
        in_specs=[pl.BlockSpec(memory_space=pl.ANY)] + [VMEM] * 6,
        out_specs=(VMEM, VMEM),
        scratch_shapes=[
            pltpu.VMEM((n, obl_dev, rows), BF16),
            pltpu.VMEM((STEPS, ns, cols, part), BF16),
            pltpu.VMEM((cols, rows), F32),
            pltpu.VMEM((nz, cols, rows), BF16),
            pltpu.VMEM((STEPS, nz, cols, rows), BF16),
            pltpu.VMEM((nz - 1, cols, rows), BF16),
            pltpu.VMEM((STEPS, nz - 1, cols, rows), BF16),
            pltpu.VMEM((cols, rows), F32),
            pltpu.VMEM((STEPS, n, rows, cols), BF16),
            pltpu.VMEM((ns, part, cols), F32),
            pltpu.VMEM((STEPS, nx, part, cols), F32),
            pltpu.VMEM((nx - 1, part, cols), F32),
            pltpu.VMEM((STEPS, nx - 1, part, cols), F32),
            pltpu.VMEM((part, cols), F32),
            pltpu.VMEM((n, 8, cols), F32),
            pltpu.VMEM((STEPS, n, 8, cols), F32),
            pltpu.VMEM((STEPS, n, 8, cols), F32),
            pltpu.VMEM((STEPS, ns, 8, cols), F32),
            pltpu.VMEM((STEPS, n, 8, cols), F32),
            pltpu.VMEM((STEPS, ns, 8, cols), F32),
            pltpu.VMEM((STEPS, ns, 8, cols), F32),
            pltpu.VMEM((STEPS, n, 8, cols), F32),
            dma((n,)),
            dma((2, n - 1)),
            dma((STEPS, 2, n - 1)),
            dma((STEPS, 2, n - 1)),
            dma((STEPS, 2, ns - 1)),
            dma((STEPS, 2, n - 1)),
            dma((STEPS, 2, ns - 1)),
            dma((STEPS, 2, ns - 1)),
            dma((STEPS, 2, n - 1)),
            dma((STEPS, 2, nz)),
            dma((STEPS, 2, nz - 1)),
            dma((STEPS, 2, nz - 1)),
            dma((STEPS, 2, nz)),
            dma((STEPS, 2, nx)),
            dma((STEPS, 2, nx - 1)),
            dma((STEPS, 2, nx - 1)),
            dma((STEPS, 2, nx)),
        ],
        compiler_params=pltpu.CompilerParams(
            collective_id=0, has_side_effects=True, vmem_limit_bytes=LIMIT
        ),
    )(idiosyncratic, factors, loadings, bars, given, eligible, holdings)


def on_device(
    factors, idiosyncratic, loadings, rating, barrier, loss_given, sector, allowed, holdings
):
    obl_dev = idiosyncratic.shape[0]
    scn_dev = idiosyncratic.shape[1]
    n = lax.axis_size("obl")
    ns = lax.axis_size("scn")
    obligors = obl_dev * n
    scenarios = scn_dev * ns
    tail_scale = 1.0 / ((1.0 - LEVEL) * scenarios)
    sector_hot = (sector[:, None] == jnp.arange(allowed.shape[1])[None, :]).astype(jnp.float32)
    eligible = lax.dot_general(
        sector_hot,
        allowed.astype(jnp.float32),
        (((1,), (1,)), ((), ())),
        precision=lax.Precision.HIGHEST,
    )
    rating_hot = (rating[:, None] == jnp.arange(barrier.shape[0])[None, :]).astype(jnp.float32)
    barrier_rows = jnp.dot(rating_hot, barrier, precision=lax.Precision.HIGHEST)
    out, short = descend(
        idiosyncratic, factors, loadings, barrier_rows[:, None], loss_given[:, None],
        eligible, holdings, n, ns, obligors, scenarios, tail_scale,
    )
    return (out.reshape(obl_dev, -1), short[:, 0, :])


def solution(mesh):
    return jax.shard_map(
        on_device,
        mesh=mesh,
        in_specs=(
            P("scn", None),
            P("obl", "scn"),
            P("obl", None),
            P("obl"),
            P(),
            P("obl"),
            P("obl"),
            P(),
            P("obl", None),
        ),
        out_specs=(P("obl", None), P()),
        check_vma=False,
    )
```

time: 591 us -> 254 us (0.43)
  waiting for transfers between devices: 389 us -> 0 us
  Pallas kernels: 0 us -> 241 us
  blocking collectives: 85.8 us -> 0 us
  matrix products: 73.4 us -> 4.78 us
  other arithmetic: 27.9 us -> 0 us
  between operations: 13.8 us -> 0.67 us
  local copies, waits for them, and re-layouts: 0.03 us -> 7.04 us
    psum x4 -> x0, waiting for transfers between devices: 389 us -> none  [the longest x2 301 us: on_device(): losses = lax.psum(partial_value, 'obl')]
    pallas_call x0 -> x1, Pallas kernels: none -> 241 us  [descend(): pl.pallas_call(functools.partial(kernel, n, ns, obligors, scenarios, tail...]
    psum x6 -> x0, blocking collectives: 85.8 us -> none  [the longest x2 42.7 us: on_device(): totals = lax.psum(jnp.sum(unnorm, 0), 'obl')]
    dot_general x5 -> x0, matrix products: 70 us -> none  [the longest x2 27.2 us: on_device(): lax.dot_general(default_prob, exposure, (((0,), (0,)), ((), ())), preferr...]
    reduce_sum x6 -> x0, other arithmetic: 24.2 us -> none  [the longest x2 10.1 us: on_device(): tail_sum = lax.psum(jnp.sum(jax.nn.softplus(scaled), 0), 'scn')]
  transfers between devices with their start and end apart: 4 -> 0, of which waited for: 4 -> 0; matrix products, arithmetic and copies ran while one was open for 2% -> 0% of each run, Pallas kernels for 0% -> 0%
where the time goes in v2:
time: 254 us
  Pallas kernels  241 us (95%)
  local copies, waits for them, and re-layouts  7.04 us (3%)
  matrix products  4.78 us (2%)
    pallas_call x1, Pallas kernels, descend(): pl.pallas_call(functools.partial(kernel, n, ns, obligors, scenarios, tail...  241 us

profile of v2, /device:TPU:0, one launch (start us, length us, event | category | flops | bytes accessed | tf_op | source)
XLA Modules:
  0.0 253.7 jit_solution(17063752755939424498)
XLA Ops:
  0.6 0.0 copy-start
  0.6 0.0 copy-start.1
  0.7 0.0 copy-start.2
  0.7 0.6 copy-done
  1.3 2.4 convolution_bitcast_fusion.bar_ref
  3.7 2.1 copy.12.given_ref
  5.8 0.0 copy-done.1
  5.8 0.0 copy-done.2
  5.8 2.4 fusion.elig_ref
  8.1 241.3 %shard_map.104 = (f32[4,512,256]{2,1,0:T(8,128)}, f32[2,8,256]{2,1,0:T(8,128)}) custom-call(bf16[2048,4096]{1,0:T(8,128)(2,1)} %idio_ref.1, bf16[4096,128]{1,0:T(8,128)(2,1)} %fact_ref.1, bf16[2048,128]{1,0:T(8,128)(2,1)} %load_ref.1, f32[2048,1]{1,0:T(8,128)} %convolution_bitcast_fusion.bar_ref, f32[2048,1]{1,0:T(8,128)} %copy.12.given_ref, ...), custom_call_target="tpu_custom_call" | custom-call | tf_op jit(solution)/shard_map/pallas_call | solution.py:322
  249.4 0.7 slice.3
  250.1 0.6 copy.15
  250.7 3.0 %copy.17 = f32[2048,256]{1,0:T(8,128)} copy(f32[2048,256]{1,0:T(8,128)} %bitcast.12) | data formatting | bytes 4194304
Async XLA Ops:
  0.6 0.7 copy-start
  0.6 5.1 %copy-start.1 = (s32[256,16]{0,1:T(8,128)S(1)}, s32[256,16]{0,1:T(8,128)}, u32[]{:S(2)}) copy-start(s32[256,16]{0,1:T(8,128)} %param.16) | copy-start | bytes 49156
  0.7 5.1 %copy-start.2 = (s32[2048]{0:T(1024)S(1)}, s32[2048]{0:T(1024)}, u32[]{:S(2)}) copy-start(s32[2048]{0:T(1024)} %param.15) | copy-start | bytes 24580

commit v3 on v2

--- a/solution.py
+++ b/solution.py
@@ -66,12 +66,13 @@
 
 def kernel(
     n, ns, obligors, scenarios, tail_scale,
-    idio_ref, fact_ref, load_ref, bar_ref, given_ref, elig_ref, hold_ref,
+    idio_ref, fact_ref, load_ref, bar_row, given_row, elig_ref, hold_ref,
     out_ref, short_ref,
     prob, expo, acc, away, near, far_out, far_in, losses, weight,
     grad, grad_near, grad_out, grad_in, pos,
     tot_buf, off_buf, sum_buf, scn_buf, tail_buf, tail_scn, new_scn, new_obl,
-    load_sem, tot_sem,
+    bar_ref, given_ref, mean_out, mean_in,
+    load_sem, tot_sem, mean_sem,
     off_sem, sum_sem, scn_sem, tail_sem, tsc_sem, nsc_sem, nob_sem,
     a_sem, b_sem, c_sem, d_sem, ga_sem, gb_sem, gc_sem, gd_sem,
 ):
@@ -109,6 +110,13 @@
     totals = spread_out(tot_buf, tot_sem.at[0], tot_sem.at[1], "obl", obl, n)
     tile = min(256, part)
 
+    @pl.loop(0, obl_dev // 128)
+    def _(t):
+        span = pl.ds(pl.multiple_of(t * 128, 128), 128)
+        bar_ref[span, :] = jnp.transpose(jnp.broadcast_to(bar_row[0:1, span], (128, 128)))
+        given_ref[span, :] = jnp.transpose(jnp.broadcast_to(given_row[0:1, span], (128, 128)))
+
+
     def probabilities(where):
         piece = order[where]
         loads[where].wait()
@@ -121,7 +129,8 @@
                 load_ref[span, :], fact, (((1,), (1,)), ((), ())), preferred_element_type=F32
             )
             latent = latent + IDIO_SCALE * prob[piece, span, :].astype(F32)
-            prob[piece, span, :] = jax.nn.sigmoid((latent - bar_ref[span, :]) * SHARP).astype(BF16)
+            half = 0.5 * jnp.tanh((latent - bar_ref[span, 0:1]) * (0.5 * SHARP))
+            prob[piece, span, :] = (0.5 + half).astype(BF16)
 
     def partial_losses(step, piece):
         acc[...] = jnp.zeros_like(acc)
@@ -152,7 +161,7 @@
     for k in range(ns):
         span = pl.ds(k * part, part)
         start = obligors * (elig_ref[span, :] * hold_ref[span, :]) / total
-        expo[0, k] = jnp.transpose(given_ref[span, :] * start / obligors).astype(BF16)
+        expo[0, k] = jnp.transpose(given_ref[span, 0:1] * start / obligors).astype(BF16)
     mine = pl.ds(pl.multiple_of(scn * part, part), part)
     pos[...] = obligors * (elig_ref[mine, :] * hold_ref[mine, :]) / total
     row = lax.broadcasted_iota(jnp.int32, (8, cols), 0)
@@ -167,6 +176,8 @@
             if step == 0 and i > 0:
                 probabilities(2 * i)
             partial_losses(step, mates[i])
+            if step > 0:
+                acc[...] *= inverse
             if i == 0:
                 offset = jnp.sum(acc[...], axis=1, keepdims=True) * (1.0 / rows)
                 off_buf[step, obl] = jnp.transpose(jnp.broadcast_to(offset, (cols, 128)))[0:8, :]
@@ -182,6 +193,8 @@
             if step == 0:
                 probabilities(2 * i + 1)
             partial_losses(step, owns[i])
+            if step > 0:
+                acc[...] *= inverse
             pair[i].wait_recv()
             value = acc[...] - offset + near[step, i].astype(F32)
             if i < nz - 1:
@@ -253,7 +266,7 @@
         final = sources[nz - 2] * 2 + 1 - inner
         final_weights = weight[step, final]
 
-        gpair, gline = [], []
+        gpair, gline, gmean = [], [], []
         for i in range(nx):
             slot = stargets[i] * 2 + 1 - sinner
             add_gradient(final, slot, final_weights, False)
@@ -267,7 +280,15 @@
             add_gradient(final, slot, final_weights, False)
             gpair[i].wait_recv()
             if i < nx - 1:
-                grad_out[i] = grad[slot] + grad_near[step, i]
+                value = grad[slot] + grad_near[step, i]
+                mean = jnp.sum(value, axis=1, keepdims=True) * (1.0 / cols)
+                mean_out[i] = jnp.transpose(jnp.broadcast_to(mean, (part, 128)))[0:8, :]
+                grad_out[i] = (value - mean).astype(BF16)
+                copy = push(
+                    mean_out.at[i], mean_in.at[step, i], mean_sem.at[step, 0, i], mean_sem.at[step, 1, i], "scn", slot
+                )
+                copy.start()
+                gmean.append(copy)
                 copy = push(
                     grad_out.at[i], grad_in.at[step, i], gb_sem.at[step, 0, i], gb_sem.at[step, 1, i], "scn", slot
                 )
@@ -278,21 +299,16 @@
         gradient = grad[scn] + grad_near[step, nx - 1]
         for i in range(nx - 1):
             gline[i].wait_recv()
-            gradient += grad_in[step, i]
-        gradient = given_ref[mine, :] * elig_ref[mine, :] * gradient
+            gmean[i].wait_recv()
+            mean = jnp.transpose(jnp.broadcast_to(mean_in[step, i, 0:1, :], (128, part)))[:, 0:1]
+            gradient += grad_in[step, i].astype(F32) + mean
+        gradient = given_ref[mine, 0:1] * elig_ref[mine, :] * gradient
         unnorm = pos[...] * jnp.exp(-STEP_RATE * gradient)
         pos[...] = unnorm
-        new_scn[step, scn] = jnp.broadcast_to(jnp.sum(unnorm, axis=0, keepdims=True), (8, cols))
-        wait_all(spread_out(new_scn.at[step], nsc_sem.at[step, 0], nsc_sem.at[step, 1], "scn", scn, ns))
-        new_obl[step, obl] = jnp.sum(new_scn[step], axis=0)
-        wait_all(spread_out(new_obl.at[step], nob_sem.at[step, 0], nob_sem.at[step, 1], "obl", obl, n))
-        total = jnp.sum(new_obl[step], axis=0)[0:1, :]
-        new = obligors * pos[...] / total
         if last:
-            out_ref[scn] = new
+            out_ref[scn] = unnorm
         else:
-            pos[...] = new
-            expo[step + 1, scn] = jnp.transpose(given_ref[mine, :] * new / obligors).astype(BF16)
+            expo[step + 1, scn] = jnp.transpose(given_ref[mine, 0:1] * unnorm).astype(BF16)
 
         def hand(slot, index, sems, peer):
             ref = out_ref.at[slot] if last else expo.at[step + 1, slot]
@@ -302,15 +318,29 @@
 
         mine_copy = hand(scn, nx - 1, gd_sem, smate)
         ggather = [hand(scn, i, gc_sem, stargets[i] * 2 + sinner) for i in range(nx - 1)]
+        new_scn[step, scn] = jnp.broadcast_to(jnp.sum(unnorm, axis=0, keepdims=True), (8, cols))
+        new_totals = spread_out(new_scn.at[step], nsc_sem.at[step, 0], nsc_sem.at[step, 1], "scn", scn, ns)
         gpassed = [mine_copy]
         for i in range(nx - 1):
             ggather[i].wait_recv()
             slot = lax.rem(souter + nx - 1 - i, nx) * 2 + sinner
             gpassed.append(hand(slot, i, gd_sem, smate))
+        wait_all(new_totals)
+        new_obl[step, obl] = jnp.sum(new_scn[step], axis=0)
+        new_totals = spread_out(new_obl.at[step], nob_sem.at[step, 0], nob_sem.at[step, 1], "obl", obl, n)
+        for copy in gpassed:
+            copy.wait_recv()
+        wait_all(new_totals)
+        total = jnp.sum(new_obl[step], axis=0)[0:1, :]
         own.wait_send()
-        for copy in pair + line + gather + passed + gpair + gline + ggather:
+        for copy in pair + line + gather + passed + gpair + gline + gmean + ggather + gpassed:
             copy.wait_send()
-        wait_all(gpassed)
+        if last:
+            for k in range(ns):
+                out_ref[k] = obligors * out_ref[k] / total
+        else:
+            pos[...] = obligors * pos[...] / total
+            inverse = jnp.transpose(jnp.broadcast_to(1.0 / total, (128, cols)))[:, 0:1]
 
 
 def descend(idiosyncratic, factors, loadings, bars, given, eligible, holdings, n, ns, obligors, scenarios, tail_scale):
@@ -339,8 +369,8 @@
             pltpu.VMEM((STEPS, n, rows, cols), BF16),
             pltpu.VMEM((ns, part, cols), F32),
             pltpu.VMEM((STEPS, nx, part, cols), F32),
-            pltpu.VMEM((nx - 1, part, cols), F32),
-            pltpu.VMEM((STEPS, nx - 1, part, cols), F32),
+            pltpu.VMEM((nx - 1, part, cols), BF16),
+            pltpu.VMEM((STEPS, nx - 1, part, cols), BF16),
             pltpu.VMEM((part, cols), F32),
             pltpu.VMEM((n, 8, cols), F32),
             pltpu.VMEM((STEPS, n, 8, cols), F32),
@@ -350,8 +380,13 @@
             pltpu.VMEM((STEPS, ns, 8, cols), F32),
             pltpu.VMEM((STEPS, ns, 8, cols), F32),
             pltpu.VMEM((STEPS, n, 8, cols), F32),
+            pltpu.VMEM((obl_dev, 128), F32),
+            pltpu.VMEM((obl_dev, 128), F32),
+            pltpu.VMEM((nx - 1, 8, part), F32),
+            pltpu.VMEM((STEPS, nx - 1, 8, part), F32),
             dma((n,)),
             dma((2, n - 1)),
+            dma((STEPS, 2, nx - 1)),
             dma((STEPS, 2, n - 1)),
             dma((STEPS, 2, n - 1)),
             dma((STEPS, 2, ns - 1)),
@@ -394,7 +429,7 @@
     rating_hot = (rating[:, None] == jnp.arange(barrier.shape[0])[None, :]).astype(jnp.float32)
     barrier_rows = jnp.dot(rating_hot, barrier, precision=lax.Precision.HIGHEST)
     out, short = descend(
-        idiosyncratic, factors, loadings, barrier_rows[:, None], loss_given[:, None],
+        idiosyncratic, factors, loadings, barrier_rows[None, :], loss_given[None, :],
         eligible, holdings, n, ns, obligors, scenarios, tail_scale,
     )
     return (out.reshape(obl_dev, -1), short[:, 0, :])

time: 254 us -> 236 us (0.929)
  Pallas kernels: 241 us -> 224 us
    pallas_call x1, Pallas kernels: 241 us -> 224 us  [descend(): pl.pallas_call(functools.partial(kernel, n, ns, obligors, scenarios, tail...]
where the time goes in v3:
time: 236 us; the launch traced here: 235 us
  Pallas kernels  224 us (95%)
  matrix products  5.1 us (2%)
  local copies, waits for them, and re-layouts  5 us (2%)
    pallas_call x1, Pallas kernels, descend(): pl.pallas_call(functools.partial(kernel, n, ns, obligors, scenarios, tail...  224 us

profile of v3, /device:TPU:0, one launch (start us, length us, event | category | flops | bytes accessed | tf_op | source)
XLA Modules:
  0.0 235.2 jit_solution(258990520108273489)
XLA Ops:
  0.6 0.0 copy-start
  0.6 0.6 copy-done
  1.3 2.0 fusion.1.bar_row
  3.3 3.1 %fusion.elig_ref = f32[2048,256]{1,0:T(8,128)} fusion(s32[2048]{0:T(1024)} %param.15, s32[256,16]{0,1:T(8,128)} %param.16), kind=kOutput, calls=%fused_computation.2 | convolution fusion | flops 100700160 | bytes 2121728 | tf_op jit(solution)/shard_map/dot_general | solution.py:423
  6.4 224.5 %shard_map.104 = (f32[4,512,256]{2,1,0:T(8,128)}, f32[2,8,256]{2,1,0:T(8,128)}) custom-call(bf16[2048,4096]{1,0:T(8,128)(2,1)} %idio_ref.1, bf16[4096,128]{1,0:T(8,128)(2,1)} %fact_ref.1, bf16[2048,128]{1,0:T(8,128)(2,1)} %load_ref.1, f32[1,2048]{1,0:T(1,128)} %fusion.1.bar_row, f32[1,2048]{1,0:T(1,128)} %bitcast.10, f32[2048,256]{1,0:T(8,128)} %fusion.elig_ref, ...), custom_call_target="tpu_custom_call" | custom-call | tf_op jit(solution)/shard_map/pallas_call | solution.py:352
  230.9 0.7 slice.3
  231.6 0.6 copy.13
  232.2 3.0 %copy.15 = f32[2048,256]{1,0:T(8,128)} copy(f32[2048,256]{1,0:T(8,128)} %bitcast.9) | data formatting | bytes 4194304
Async XLA Ops:
  0.6 0.7 copy-start
